TPU v7x, 32 devices: a whole 2x2x4 slice. The times are simulated.
32 devices in a mesh: groups: 2 (over y), field: 4 (over x, core), wave: 4 (over z).
Axes of the slice: x: 2, y: 2, z: 4, core: 2. Of those that a mesh axis runs over, the one named last changes fastest.
Arguments:
- mode_basis: bfloat16 [22, 512, 512], P(None, 'wave'), may hold values from -6 to 6
- coef_table: bfloat16 [4096, 22], replicated, may hold values from -1.5 to 1.5
- table_index: int32 [64], P(('groups', 'field')), parts along dimension 0, may hold values from 0 to 4095
- wave_lengths: float32 [8], P('wave'), may hold values from 0.32 to 1.05
- sed_table: float32 [1024, 8], replicated, may hold values from 0.05 to 1
- template_ids: int32 [64, 8], P(('groups', 'field')), parts along dimension 0, may hold values from 0 to 1023
Outputs:
- mixed: bfloat16 [64, 8, 256, 256], P(('groups', 'field'), None, 'wave'), parts along dimension 0
There are 2 independent parts, one for each index of `groups`. A program takes and returns all parts, laid end to end along the dimension named above; an argument that names none is the same for every part. Nothing has to cross between parts.
All inputs are finite; a program needn't handle non-finite values.
Results may differ from a plain program's by a relative error of at most 0.0065.
Values may be sent and summed in bfloat16 or wider, within the bound.
A program may use at most 128 MiB of HBM per device.

v0:
```python
import math
import jax
import jax.numpy as jnp
from jax import lax
from jax.sharding import PartitionSpec as P

PUP = 512
PIX = 256
TWO_PI = 2.0 * math.pi
SAMPLING = 0.25
EPSILON = 1e-06


def transform_table(wave_lengths, pixels, pupil_side):
    pixel_offset = jnp.arange(pixels, dtype=jnp.int32) - pixels // 2
    pupil_offset = 2 * jnp.arange(pupil_side, dtype=jnp.int32) - pupil_side + 1
    products = (pixel_offset[:, None] * pupil_offset[None, :]).astype(jnp.float32)
    factor = TWO_PI * SAMPLING / (2.0 * pupil_side) / wave_lengths
    angles = products[None, :, :] * factor[:, None, None]
    cosine = jnp.cos(angles)
    sine_part = jnp.sin(angles)
    upper_half = jnp.concatenate([cosine, sine_part], axis=2)
    lower_half = jnp.concatenate([-sine_part, cosine], axis=2)
    return jnp.concatenate([upper_half, lower_half], axis=1).astype(jnp.bfloat16)


def aperture_rows(row_start, row_count, pupil_side):
    row_pos = 2 * (row_start + jnp.arange(row_count, dtype=jnp.int32)) - pupil_side + 1
    col_pos = 2 * jnp.arange(pupil_side, dtype=jnp.int32) - pupil_side + 1
    radius_sq = row_pos[:, None] * row_pos[:, None] + col_pos[None, :] * col_pos[None, :]
    inner_edge = 61 * pupil_side // 100
    inside = (radius_sq <= pupil_side * pupil_side) & (radius_sq >= inner_edge * inner_edge)
    return inside.astype(jnp.float32)


def pupil_section(path_rows, wave_lengths, kernel_table, row_start):
    row_count = path_rows.shape[1]
    pupil_side = path_rows.shape[2]
    opening = aperture_rows(row_start, row_count, pupil_side)
    phase_map = path_rows[:, None, :, :] * (TWO_PI / wave_lengths)[None, :, None, None]
    field_real = opening * jnp.cos(phase_map)
    field_imag = opening * jnp.sin(phase_map)
    pupil_field = jnp.concatenate([field_real, field_imag], axis=3).astype(jnp.bfloat16)
    first_pass = jnp.einsum(
        "flxy,luy->flxu", pupil_field, kernel_table, preferred_element_type=jnp.float32
    )
    return first_pass.astype(jnp.bfloat16)


def finish_section(first_pass, kernel_table):
    pixels = first_pass.shape[3] // 2
    stacked = jnp.concatenate([first_pass[..., :pixels], first_pass[..., pixels:]], axis=2)
    image_field = jnp.einsum(
        "lux,flxv->fluv", kernel_table, stacked, preferred_element_type=jnp.float32
    )
    intensity = (
        image_field[:, :, :pixels] * image_field[:, :, :pixels]
        + image_field[:, :, pixels:] * image_field[:, :, pixels:]
    )
    mean_level = jnp.mean(intensity, axis=(2, 3), keepdims=True)
    return (intensity / (mean_level + EPSILON)).astype(jnp.bfloat16)


def local(mode_basis, coef_table, table_index, wave_lengths, sed_table, template_ids):
    kernel_table = transform_table(wave_lengths, PIX, PUP)
    table_rows = coef_table.shape[0]
    selector = (table_index[:, None] == jnp.arange(table_rows, dtype=jnp.int32)[None, :]).astype(
        jnp.bfloat16
    )
    coeffs = jnp.dot(selector, coef_table, preferred_element_type=jnp.float32).astype(jnp.bfloat16)
    mode_count = mode_basis.shape[0]
    positions = coeffs.shape[0]
    whole_basis = lax.all_gather(mode_basis, "wave", axis=1, tiled=True)
    path_diff = jnp.dot(
        coeffs, whole_basis.reshape(mode_count, -1), preferred_element_type=jnp.float32
    )
    path_diff = path_diff.reshape(positions, PUP, PUP)
    first_pass = pupil_section(path_diff, wave_lengths, kernel_table, 0)
    spectra = finish_section(first_pass, kernel_table)
    pixel_slabs = lax.all_to_all(spectra, "wave", split_axis=2, concat_axis=1, tiled=True)
    sed_rows = sed_table.shape[0]
    one_hot = (
        template_ids[:, :, None] == jnp.arange(sed_rows, dtype=jnp.int32)[None, None, :]
    ).astype(jnp.float32)
    raw_weights = jnp.einsum("fjn,nl->fjl", one_hot, sed_table, precision=lax.Precision.HIGHEST)
    weights = (raw_weights / jnp.sum(raw_weights, axis=2, keepdims=True)).astype(jnp.bfloat16)
    mixed = jnp.einsum("fjl,flrp->fjrp", weights, pixel_slabs, preferred_element_type=jnp.float32)
    return mixed.astype(jnp.bfloat16)


def solution(mesh):
    return jax.shard_map(
        local,
        mesh=mesh,
        in_specs=(
            P(None, "wave", None),
            P(),
            P(("groups", "field")),
            P("wave"),
            P(),
            P(("groups", "field"), None),
        ),
        out_specs=P(("groups", "field"), None, "wave", None),
        check_vma=False,
    )
```

profile of v0, /device:TPU:0, one launch (start us, length us, event | category | flops | bytes accessed | tf_op | source)
XLA Modules:
  0.0 431.0 jit_solution(3552195632405545953)
XLA Ops:
  6.5 0.0 copy-start
  6.5 0.0 all-gather.2.cloned.1.call-start
  6.5 0.7 all-gather.2.cloned.1.call-update
  7.3 0.7 broadcast_divide_fusion.1
  8.0 0.1 multiply_convert_fusion
  8.1 0.2 fusion.30
  8.3 4.1 fusion.22
  12.4 0.0 copy-start.3
  12.4 200.3 %all-gather.2.cloned.1.call-done = bf16[22,512,512]{2,1,0:T(8,128)(2,1)} async-done(((bf16[22,128,512]{2,1,0:T(8,128)(2,1)}), bf16[22,512,512]{2,1,0:T(8,128)(2,1)}) %all-gather.2.cloned.1.call-update) | async-done | bytes 11534352 | tf_op jit(solution)/shard_map/all_gather | solution.py:73
  212.7 10.0 %slice_bitcast_fusion = bf16[512,512,22]{1,0,2:T(8,128)(2,1)} fusion(bf16[22,512,512]{2,1,0:T(8,128)(2,1)} %all-gather.2.cloned.1.call-done), kind=kLoop, calls=%fused_computation.13 | loop fusion | bytes 23068672 | tf_op jit(solution)/shard_map/reshape.39
  222.7 0.0 copy-done
  222.7 0.0 copy-done.3
  222.7 24.2 %fusion.9 = f32[8,512,512]{2,0,1:T(8,128)} fusion(bf16[512,512,22]{1,0,2:T(8,128)(2,1)} %slice_bitcast_fusion, bf16[4096,22]{0,1:T(8,128)(2,1)S(1)} %copy-done, s32[8]{0:T(128)S(1)} %copy-done.3), kind=kOutput, calls=%fused_computation.11 | convolution fusion | flops 93749424 | bytes 20103200 | tf_op jit(solution)/shard_map/dot_general | solution.py:74
  247.0 8.2 %copy.20 = f32[8,512,512]{2,1,0:T(8,128)S(1)} copy(f32[8,512,512]{2,0,1:T(8,128)} %fusion.9) | data formatting | bytes 16777216 | tf_op jit(solution)/shard_map/dot_general | solution.py:74
  255.2 64.3 %fusion.2 = (bf16[8,2,512,512]{3,2,0,1:T(8,128)(2,1)}, bf16[8,2,512,512]{3,2,0,1:T(8,128)(2,1)}) fusion(f32[2]{0:T(128)S(1)} %get-tuple-element.13, f32[8,512,512]{2,1,0:T(8,128)S(1)} %copy.20, f32[512,512]{1,0:T(8,128)S(1)} %fusion.30), kind=kLoop, calls=%fused_computation.4 | loop fusion | flops 20971520 | bytes 26214408 | tf_op jit(solution)/shard_map/convert
  319.5 14.6 %convert_bitcast_fusion = bf16[8,2,512,512]{3,2,0,1:T(8,128)(2,1)} fusion(bf16[8,2,512,512]{3,2,0,1:T(8,128)(2,1)} %get-tuple-element.6, bf16[8,2,512,512]{3,2,0,1:T(8,128)(2,1)} %get-tuple-element.5, bf16[2,256,512]{2,1,0:T(8,128)(2,1)S(1)} %get-tuple-element.11, bf16[2,256,512]{2,1,0:T(8,128)(2,1)S(1)} %get-tuple-element.10, ...), kind=kOutput, calls=%fused_computation.18 | convolution fusion | flops 8636071936 | bytes 26738688 | tf_op jit(solution)/shard_map/flxy,luy->flxu/dot_general | solution.py:44
  334.1 5.8 %fusion.41 = (bf16[8,2,512,256]{3,2,0,1:T(8,128)(2,1)}, bf16[8,2,512,256]{3,2,0,1:T(8,128)(2,1)}) fusion(bf16[8,2,512,512]{3,2,0,1:T(8,128)(2,1)} %convert_bitcast_fusion), kind=kLoop, calls=%fused_computation.58 | loop fusion | bytes 16777216 | tf_op jit(solution)/shard_map/slice | solution.py:52
  339.9 11.0 %fusion.18 = f32[8,2,512,256]{2,3,0,1:T(8,128)} fusion(bf16[8,2,512,256]{3,2,0,1:T(8,128)(2,1)} %get-tuple-element.8, bf16[8,2,512,256]{3,2,0,1:T(8,128)(2,1)} %get-tuple-element.7, bf16[2,256,512]{2,1,0:T(8,128)(2,1)S(1)} %get-tuple-element.11, bf16[2,256,512]{2,1,0:T(8,128)(2,1)S(1)} %get-tuple-element.10, bf16[2,256,512]{2,1,0:T(8,128)(2,1)S(1)} %get-tuple-element.9), kind=kOutput, calls=%fused_computation.23 | convolution fusion | flops 4320133120 | bytes 18350080 | tf_op jit(solution)/shard_map/lux,flxv->fluv/dot_general | solution.py:53
  351.0 4.3 fusion.31
  355.3 1.6 copy-done.2
  356.8 0.8 divide_convert_fusion
  357.6 0.0 copy-start.4
  357.6 0.0 copy-start.5
  357.6 3.1 copy.22
  360.7 3.6 all-to-all-start
  364.3 0.0 copy-done.4
  364.3 1.0 fusion.32
  365.4 47.6 %all-to-all-done = bf16[8,2,256,256]{3,0,1,2:T(8,128)(2,1)S(1)} async-done(((bf16[8,2,256,256]{3,0,1,2:T(8,128)(2,1)}), bf16[8,2,256,256]{3,0,1,2:T(8,128)(2,1)S(1)}, u32[]{:S(2)}, u32[]{:S(2)}) %all-to-all-start) | async-done | bytes 2097184 | tf_op jit(solution)/shard_map/all_to_all | solution.py:80
  413.0 2.9 copy.24
  415.9 2.8 all_to_all.16
  418.7 2.0 convolution_convert_fusion
  420.7 3.5 copy.26
  (8 shorter events, 0.0 us)
Async XLA Ops:
  6.5 216.2 %copy-start = (bf16[4096,22]{0,1:T(8,128)(2,1)S(1)}, bf16[4096,22]{0,1:T(8,128)(2,1)}, u32[]{:S(2)}) copy-start(bf16[4096,22]{0,1:T(8,128)(2,1)} %param.7) | copy-start | bytes 540676
  6.5 206.2 %all-gather.2.cloned.1.call-start = ((), (), s32[]{:S(2)}) async-start(), calls=%async_computation.1 | async-start | bytes 14417920 | tf_op jit(solution)/shard_map/all_gather | solution.py:73
  12.4 210.3 %copy-start.3 = (s32[8]{0:T(128)S(1)}, s32[8]{0:T(128)}, u32[]{:S(2)}) copy-start(s32[8]{0:T(128)} %param.8) | copy-start | bytes 100
  351.0 5.8 %copy-start.2 = (f32[8,2,512,256]{2,3,0,1:T(8,128)S(1)}, f32[8,2,512,256]{2,3,0,1:T(8,128)}, u32[]{:S(2)}) copy-start(f32[8,2,512,256]{2,3,0,1:T(8,128)} %fusion.18) | copy-start | bytes 25165828
  357.6 6.7 %copy-start.4 = (f32[1024,8]{0,1:T(8,128)S(1)}, f32[1024,8]{0,1:T(8,128)}, u32[]{:S(2)}) copy-start(f32[1024,8]{0,1:T(8,128)} %param.10) | copy-start | bytes 98308
  357.6 6.7 %copy-start.5 = (s32[8,8]{1,0:T(8,128)S(1)}, s32[8,8]{1,0:T(8,128)}, u32[]{:S(2)}) copy-start(s32[8,8]{1,0:T(8,128)} %param.11) | copy-start | bytes 772
  360.7 52.3 %all-to-all-start = ((bf16[8,2,256,256]{3,0,1,2:T(8,128)(2,1)}), bf16[8,2,256,256]{3,0,1,2:T(8,128)(2,1)S(1)}, u32[]{:S(2)}, u32[]{:S(2)}) async-start(bf16[8,2,256,256]{3,0,1,2:T(8,128)(2,1)} %copy.22), calls=%async_computation | async-start | bytes 4194304 | tf_op jit(solution)/shard_map/all_to_all | solution.py:80
  415.9 8.3 %copy-start.1 = (bf16[4096,22]{0,1:T(8,128)(2,1)S(1)}, bf16[4096,22]{0,1:T(8,128)(2,1)}, u32[]{:S(2)}) copy-start(bf16[4096,22]{0,1:T(8,128)(2,1)} %param.7) | copy-start | bytes 540676
Sparse Core Ops, SparseCore 0:
  8.9 203.7 all-gather.1
where the time goes:
time: 431 us
  waiting for transfers between devices  249 us (58%)
  other arithmetic  74.5 us (17%)
  matrix products  52.9 us (12%)
  local copies, waits for them, and re-layouts  37.8 us (9%)
  between operations  13.5 us (3%)
    all_gather x1, waiting for transfers between devices, local(): whole_basis = lax.all_gather(mode_basis, 'wave', axis=1, tiled=True)  200 us
    another operation x2, other arithmetic  68.4 us
    all_to_all x1, waiting for transfers between devices, local(): lax.all_to_all(spectra, 'wave', split_axis=2, concat_axis=1, tiled=True)  47.6 us
    dot_general x1, matrix products, local(): jnp.dot(coeffs, whole_basis.reshape(mode_count, -1), preferred_element_ty...  24.2 us
    dot_general x1, matrix products, pupil_section(): jnp.einsum('flxy,luy->flxu', pupil_field, kernel_table, preferred_element...  14.6 us
    dot_general x1, matrix products, finish_section(): jnp.einsum('lux,flxv->fluv', kernel_table, stacked, preferred_element_typ...  11 us
    another operation x1, local copies, waits for them, and re-layouts  9.99 us
  transfers between devices with their start and end apart: 2, of which 2 were waited for; matrix products, arithmetic and copies ran while one was open for 1% of the time, Pallas kernels for 0%

commit v1 on v0

--- a/solution.py
+++ b/solution.py
@@ -77,7 +77,9 @@
     path_diff = path_diff.reshape(positions, PUP, PUP)
     first_pass = pupil_section(path_diff, wave_lengths, kernel_table, 0)
     spectra = finish_section(first_pass, kernel_table)
-    pixel_slabs = lax.all_to_all(spectra, "wave", split_axis=2, concat_axis=1, tiled=True)
+    pieces = jnp.split(spectra, lax.axis_size("wave"), axis=2)
+    received = lax.all_to_all(jnp.stack(pieces), "wave", 0, 0)
+    pixel_slabs = jnp.concatenate(received, axis=1)
     sed_rows = sed_table.shape[0]
     one_hot = (
         template_ids[:, :, None] == jnp.arange(sed_rows, dtype=jnp.int32)[None, None, :]

time: 431 us -> 437 us (1.014)
    reshape x0 -> x2, local copies, waits for them, and re-layouts: none -> 6.26 us  [local(): pixel_slabs = jnp.concatenate(received, axis=1)]
    another operation x1 -> x3, local copies, waits for them, and re-layouts: 9.99 us -> 15.9 us
    all_to_all x2 -> x0, local copies, waits for them, and re-layouts: 5.72 us -> none  [local(): lax.all_to_all(spectra, 'wave', split_axis=2, concat_axis=1, tiled=True)]
    another operation x2 -> x3, other arithmetic: 68.4 us -> 70.9 us
where the time goes in v1:
time: 437 us
  waiting for transfers between devices  249 us (57%)
  other arithmetic  77 us (18%)
  matrix products  52.9 us (12%)
  local copies, waits for them, and re-layouts  41.3 us (9%)
  between operations  13.5 us (3%)
    all_gather x1, waiting for transfers between devices, local(): whole_basis = lax.all_gather(mode_basis, 'wave', axis=1, tiled=True)  200 us
    another operation x2, other arithmetic  68.4 us
    all_to_all x1, waiting for transfers between devices, local(): received = lax.all_to_all(jnp.stack(pieces), 'wave', 0, 0)  47.6 us
    dot_general x1, matrix products, local(): jnp.dot(coeffs, whole_basis.reshape(mode_count, -1), preferred_element_ty...  24.2 us
    dot_general x1, matrix products, pupil_section(): jnp.einsum('flxy,luy->flxu', pupil_field, kernel_table, preferred_element...  14.6 us
    dot_general x1, matrix products, finish_section(): jnp.einsum('lux,flxv->fluv', kernel_table, stacked, preferred_element_typ...  11 us
    another operation x1, local copies, waits for them, and re-layouts  9.99 us
  transfers between devices with their start and end apart: 2, of which 2 were waited for; matrix products, arithmetic and copies ran while one was open for 1% of the time, Pallas kernels for 0%

profile of v1, /device:TPU:0, one launch (start us, length us, event | category | flops | bytes accessed | tf_op | source)
XLA Modules:
  0.0 436.9 jit_solution(1968816101486275504)
XLA Ops:
  6.5 0.0 copy-start
  6.5 0.0 all-gather.2.cloned.1.call-start
  6.5 0.7 all-gather.2.cloned.1.call-update
  7.3 0.7 broadcast_divide_fusion.1
  8.0 0.1 multiply_convert_fusion
  8.1 0.2 fusion.30
  8.3 4.1 fusion.22
  12.4 0.0 copy-start.3
  12.4 200.3 %all-gather.2.cloned.1.call-done = bf16[22,512,512]{2,1,0:T(8,128)(2,1)} async-done(((bf16[22,128,512]{2,1,0:T(8,128)(2,1)}), bf16[22,512,512]{2,1,0:T(8,128)(2,1)}) %all-gather.2.cloned.1.call-update) | async-done | bytes 11534352 | tf_op jit(solution)/shard_map/all_gather | solution.py:73
  212.7 10.0 %slice_bitcast_fusion = bf16[512,512,22]{1,0,2:T(8,128)(2,1)} fusion(bf16[22,512,512]{2,1,0:T(8,128)(2,1)} %all-gather.2.cloned.1.call-done), kind=kLoop, calls=%fused_computation.13 | loop fusion | bytes 23068672 | tf_op jit(solution)/shard_map/reshape.41
  222.7 0.0 copy-done
  222.7 0.0 copy-done.3
  222.7 24.2 %fusion.9 = f32[8,512,512]{2,0,1:T(8,128)} fusion(bf16[512,512,22]{1,0,2:T(8,128)(2,1)} %slice_bitcast_fusion, bf16[4096,22]{0,1:T(8,128)(2,1)S(1)} %copy-done, s32[8]{0:T(128)S(1)} %copy-done.3), kind=kOutput, calls=%fused_computation.11 | convolution fusion | flops 93749424 | bytes 20103200 | tf_op jit(solution)/shard_map/dot_general | solution.py:74
  246.9 8.2 %copy.19 = f32[8,512,512]{2,1,0:T(8,128)S(1)} copy(f32[8,512,512]{2,0,1:T(8,128)} %fusion.9) | data formatting | bytes 16777216 | tf_op jit(solution)/shard_map/dot_general | solution.py:74
  255.2 64.3 %fusion.2 = (bf16[8,2,512,512]{3,2,0,1:T(8,128)(2,1)}, bf16[8,2,512,512]{3,2,0,1:T(8,128)(2,1)}) fusion(f32[2]{0:T(128)S(1)} %get-tuple-element.17, f32[8,512,512]{2,1,0:T(8,128)S(1)} %copy.19, f32[512,512]{1,0:T(8,128)S(1)} %fusion.30), kind=kLoop, calls=%fused_computation.4 | loop fusion | flops 20971520 | bytes 26214408 | tf_op jit(solution)/shard_map/convert
  319.5 14.6 %convert_bitcast_fusion = bf16[8,2,512,512]{3,2,0,1:T(8,128)(2,1)} fusion(bf16[8,2,512,512]{3,2,0,1:T(8,128)(2,1)} %get-tuple-element.6, bf16[8,2,512,512]{3,2,0,1:T(8,128)(2,1)} %get-tuple-element.5, bf16[2,256,512]{2,1,0:T(8,128)(2,1)S(1)} %get-tuple-element.15, bf16[2,256,512]{2,1,0:T(8,128)(2,1)S(1)} %get-tuple-element.14, ...), kind=kOutput, calls=%fused_computation.18 | convolution fusion | flops 8636071936 | bytes 26738688 | tf_op jit(solution)/shard_map/flxy,luy->flxu/dot_general | solution.py:44
  334.1 5.8 %fusion.41 = (bf16[8,2,512,256]{3,2,0,1:T(8,128)(2,1)}, bf16[8,2,512,256]{3,2,0,1:T(8,128)(2,1)}) fusion(bf16[8,2,512,512]{3,2,0,1:T(8,128)(2,1)} %convert_bitcast_fusion), kind=kLoop, calls=%fused_computation.63 | loop fusion | bytes 16777216 | tf_op jit(solution)/shard_map/slice | solution.py:52
  339.9 11.0 %fusion.18 = f32[8,2,512,256]{2,3,0,1:T(8,128)} fusion(bf16[8,2,512,256]{3,2,0,1:T(8,128)(2,1)} %get-tuple-element.8, bf16[8,2,512,256]{3,2,0,1:T(8,128)(2,1)} %get-tuple-element.7, bf16[2,256,512]{2,1,0:T(8,128)(2,1)S(1)} %get-tuple-element.15, bf16[2,256,512]{2,1,0:T(8,128)(2,1)S(1)} %get-tuple-element.14, bf16[2,256,512]{2,1,0:T(8,128)(2,1)S(1)} %get-tuple-element.13), kind=kOutput, calls=%fused_computation.24 | convolution fusion | flops 4320133120 | bytes 18350080 | tf_op jit(solution)/shard_map/lux,flxv->fluv/dot_general | solution.py:53
  350.9 4.3 fusion.31
  355.2 1.6 copy-done.2
  356.8 0.8 divide_convert_fusion
  357.6 1.2 slice_bitcast_fusion.4
  358.7 2.5 pad_maximum_fusion
  361.3 4.8 %copy.21 = bf16[4,8,2,64,256]{4,3,2,1,0:T(8,128)(2,1)} copy(bf16[4,8,2,64,256]{3,4,1,2,0:T(8,128)(2,1)} %pad_maximum_fusion) | data formatting | bytes 4194304 | tf_op jit(solution)/shard_map/stack | solution.py:81
  366.0 3.6 all-to-all-start
  369.6 0.0 copy-done.4
  369.7 1.0 fusion.32
  370.7 47.6 %all-to-all-done = bf16[4,8,2,64,256]{4,3,2,1,0:T(8,128)(2,1)S(1)} async-done(((bf16[4,8,2,64,256]{4,3,2,1,0:T(8,128)(2,1)}), bf16[4,8,2,64,256]{4,3,2,1,0:T(8,128)(2,1)S(1)}, u32[]{:S(2)}, u32[]{:S(2)}) %all-to-all-start) | async-done | bytes 2097184 | tf_op jit(solution)/shard_map/all_to_all | solution.py:81
  418.3 3.5 copy.22
  421.8 2.8 reshape.109
  424.6 2.0 convolution_convert_fusion
  426.6 3.5 copy.24
  (10 shorter events, 0.0 us)
Async XLA Ops:
  6.5 216.2 %copy-start = (bf16[4096,22]{0,1:T(8,128)(2,1)S(1)}, bf16[4096,22]{0,1:T(8,128)(2,1)}, u32[]{:S(2)}) copy-start(bf16[4096,22]{0,1:T(8,128)(2,1)} %param.7) | copy-start | bytes 540676
  6.5 206.2 %all-gather.2.cloned.1.call-start = ((), (), s32[]{:S(2)}) async-start(), calls=%async_computation.1 | async-start | bytes 14417920 | tf_op jit(solution)/shard_map/all_gather | solution.py:73
  12.4 210.3 %copy-start.3 = (s32[8]{0:T(128)S(1)}, s32[8]{0:T(128)}, u32[]{:S(2)}) copy-start(s32[8]{0:T(128)} %param.8) | copy-start | bytes 100
  350.9 5.8 %copy-start.2 = (f32[8,2,512,256]{2,3,0,1:T(8,128)S(1)}, f32[8,2,512,256]{2,3,0,1:T(8,128)}, u32[]{:S(2)}) copy-start(f32[8,2,512,256]{2,3,0,1:T(8,128)} %fusion.18) | copy-start | bytes 25165828
  361.2 8.4 %copy-start.4 = (f32[1024,8]{0,1:T(8,128)S(1)}, f32[1024,8]{0,1:T(8,128)}, u32[]{:S(2)}) copy-start(f32[1024,8]{0,1:T(8,128)} %param.10) | copy-start | bytes 98308
  361.3 8.4 %copy-start.5 = (s32[8,8]{1,0:T(8,128)S(1)}, s32[8,8]{1,0:T(8,128)}, u32[]{:S(2)}) copy-start(s32[8,8]{1,0:T(8,128)} %param.11) | copy-start | bytes 772
  366.0 52.3 %all-to-all-start = ((bf16[4,8,2,64,256]{4,3,2,1,0:T(8,128)(2,1)}), bf16[4,8,2,64,256]{4,3,2,1,0:T(8,128)(2,1)S(1)}, u32[]{:S(2)}, u32[]{:S(2)}) async-start(bf16[4,8,2,64,256]{4,3,2,1,0:T(8,128)(2,1)} %copy.21), calls=%async_computation | async-start | bytes 4194304 | tf_op jit(solution)/shard_map/all_to_all | solution.py:81
  421.8 8.3 %copy-start.1 = (bf16[4096,22]{0,1:T(8,128)(2,1)S(1)}, bf16[4096,22]{0,1:T(8,128)(2,1)}, u32[]{:S(2)}) copy-start(bf16[4096,22]{0,1:T(8,128)(2,1)} %param.7) | copy-start | bytes 540676
Sparse Core Ops, SparseCore 0:
  8.9 203.7 all-gather.1
